TPU v7x, 32 devices: a whole 2x2x4 slice. The times are simulated.
32 devices in a mesh: seq: 8 (over y, x, core), tp: 4 (over z).
Axes of the slice: x: 2, y: 2, z: 4, core: 2. Of those that a mesh axis runs over, the one named last changes fastest.
Arguments:
- patches: bfloat16 [4096, 1280], P('seq'), may hold values from -6 to 6
- image_ids: int32 [1024], replicated, may hold values from 0 to 15, never falling along the last dimension, each value on 1 to 128 neighbouring positions
- vision_gain: float32 [1280], replicated, may hold values from 0.5 to 2
- v_query: bfloat16 [1280, 1280], P(None, 'tp'), may hold values from -0.15625 to 0.15625
- v_key: bfloat16 [1280, 1280], P(None, 'tp'), may hold values from -0.15625 to 0.15625
- v_value: bfloat16 [1280, 1280], P(None, 'tp'), may hold values from -0.15625 to 0.15625
- v_out: bfloat16 [1280, 1280], P('tp'), may hold values from -0.625 to 0.625
- merge_gain: float32 [1280], replicated, may hold values from 0.5 to 1.5
- merge_up: bfloat16 [5120, 5120], P('seq', 'tp'), may hold values from -0.078125 to 0.078125
- merge_down: bfloat16 [5120, 8192], P('tp', 'seq'), may hold values from -0.078125 to 0.078125
- owners: int32 [1024, 1], replicated, may hold values from 0 to 7; in each aligned block of 128 rows (0 to 127, 128 to 255, ...) at most 32 rows name the same one
- text_embed: bfloat16 [2048, 8192], P('seq', 'tp'), may hold values from -6 to 6
- segment_ids: int32 [2048], P('seq'), may hold values from 0 to 31, never falling along the last dimension, each value on 1 to 256 neighbouring positions
- lang_gain: float32 [8192], replicated, may hold values from 0.5 to 2
- l_query: bfloat16 [8192, 4096], P(None, 'tp'), may hold values from -0.0625 to 0.0625
- l_key: bfloat16 [8192, 1024], P(None, 'tp'), may hold values from -0.0625 to 0.0625
- l_value: bfloat16 [8192, 1024], P(None, 'tp'), may hold values from -0.0625 to 0.0625
- l_out: bfloat16 [4096, 8192], P('tp'), may hold values from -0.09375 to 0.09375
Outputs:
- layer_out: bfloat16 [2048, 8192], P('seq', 'tp')
Inputs may be any that keep to these rules, and one draw needn't show every extreme that they name: `image_ids`: never falling; each image spans 1 to 128 merged tokens, one exactly 128. `owners`: among the rows of one device (aligned blocks of 128 rows) at most 32 name the same packed sequence. `segment_ids`: never falling; each document holds 1 to 256 slots, one exactly 256.
All inputs are finite; a program needn't handle non-finite values.
Results may differ from a plain program's by a relative error of at most 0.019.
Values may be sent and summed in bfloat16 or wider, within the bound.
A program may use at most 128 MiB of HBM per device.

v0:
```python
import math

import jax
import jax.numpy as jnp
from jax import lax
from jax.sharding import PartitionSpec as P

DV = 1280
VHEADS = 16
LHD = 128


EPSILON = 1e-06
NEG_FILL = -1e30


def extended(cells, sides, width):
    for axis, dim in sides:
        count = lax.axis_size(axis)
        ends = count - 1
        head = lax.slice_in_dim(cells, 0, width, axis=dim)
        tail = lax.slice_in_dim(cells, cells.shape[dim] - width, cells.shape[dim], axis=dim)
        cells = jnp.concatenate(
            [
                lax.ppermute(tail, axis, [(i, (i + 1) % count) for i in range(ends)]),
                cells,
                lax.ppermute(head, axis, [((i + 1) % count, i) for i in range(ends)]),
            ],
            axis=dim,
        )
    return cells


def rms_scaled(values, norm_gain):
    mean_square = jnp.mean(values * values, axis=-1, keepdims=True)
    return (values * lax.rsqrt(mean_square + EPSILON) * norm_gain).astype(jnp.bfloat16)


def masked_attend(query_rows, key_rows, value_rows, allowed, score_scale):
    scores = (
        jnp.einsum("qhd,nhd->hqn", query_rows, key_rows, preferred_element_type=jnp.float32)
        * score_scale
    )
    scores = jnp.where(allowed[None], scores, NEG_FILL)
    highest = jnp.max(scores, axis=-1, keepdims=True)
    weights_raw = jnp.where(allowed[None], jnp.exp(scores - highest), 0.0)
    totals = jnp.sum(weights_raw, axis=-1)
    mixed = jnp.einsum(
        "hqn,nhd->qhd",
        weights_raw.astype(jnp.bfloat16),
        value_rows,
        preferred_element_type=jnp.float32,
    )
    mixed = mixed / jnp.transpose(totals)[:, :, None]
    return mixed.reshape(mixed.shape[0], -1).astype(jnp.bfloat16)


def body(
    patches,
    image_ids,
    vision_gain,
    v_query,
    v_key,
    v_value,
    v_out,
    merge_gain,
    merge_up,
    merge_down,
    owners,
    text_embed,
    segment_ids,
    lang_gain,
    l_query,
    l_key,
    l_value,
    l_out,
):
    row_count = patches.shape[0]
    local_width = v_query.shape[1]
    head_size = DV // VHEADS
    head_count = local_width // head_size
    score_scale = 1.0 / math.sqrt(head_size)
    seq_index = lax.axis_index("seq")
    patch_ids = jnp.repeat(image_ids, 4)
    my_ids = lax.dynamic_slice_in_dim(patch_ids, seq_index * row_count, row_count)
    vision_state = patches.astype(jnp.float32)
    normed = rms_scaled(vision_state, vision_gain)
    query_rows = jnp.dot(normed, v_query, preferred_element_type=jnp.float32).astype(jnp.bfloat16)
    key_part = jnp.dot(normed, v_key, preferred_element_type=jnp.float32).astype(jnp.bfloat16)
    value_part = jnp.dot(normed, v_value, preferred_element_type=jnp.float32).astype(jnp.bfloat16)
    key_value = jnp.concatenate([key_part, value_part], axis=1)
    query_grid = query_rows.reshape(row_count, head_count, head_size)
    nearby = extended(key_value, (("seq", 0),), row_count)
    padded_ids = jnp.pad(patch_ids, (row_count, row_count), constant_values=-1)
    nearby_ids = lax.dynamic_slice_in_dim(padded_ids, seq_index * row_count, 3 * row_count)
    allowed = my_ids[:, None] == nearby_ids[None, :]
    nearby_keys = nearby[:, :local_width].reshape(3 * row_count, head_count, head_size)
    nearby_values = nearby[:, local_width:].reshape(3 * row_count, head_count, head_size)
    attended = masked_attend(query_grid, nearby_keys, nearby_values, allowed, score_scale)
    partial_value = jnp.dot(attended, v_out, preferred_element_type=jnp.float32)
    summed = lax.psum(partial_value.astype(jnp.bfloat16), "tp").astype(jnp.float32)
    merge_normed = rms_scaled(vision_state + summed, merge_gain)
    token_count = row_count // 4
    merge_rows = merge_normed.reshape(token_count, 4 * DV)
    hidden_sum = jnp.dot(
        merge_rows,
        lax.all_gather(merge_up, "seq", axis=0, tiled=True),
        preferred_element_type=jnp.float32,
    )
    hidden = jax.nn.gelu(hidden_sum, approximate=False).astype(jnp.bfloat16)
    down_terms = jnp.dot(
        hidden,
        lax.all_gather(merge_down, "seq", axis=1, tiled=True),
        preferred_element_type=jnp.float32,
    )
    merged = lax.psum_scatter(
        down_terms.astype(jnp.bfloat16), "tp", scatter_dimension=1, tiled=True
    )
    owner_count = lax.axis_size("seq")
    pair_cap = 2 * token_count // owner_count
    feature_width = merged.shape[1]
    owner_iota = jnp.arange(owner_count, dtype=jnp.int32)
    destination = owners[:, 0]
    one_hot = (destination[:, None] == owner_iota[None, :]).astype(jnp.int32)
    grid_counts = one_hot.reshape(owner_count, token_count, owner_count)
    pair_counts = jnp.sum(grid_counts, axis=1)
    mine = lax.dynamic_slice_in_dim(grid_counts, seq_index, 1, 0)[0]
    local_rank = jnp.sum((jnp.cumsum(mine, axis=0) - mine) * mine, axis=1)
    my_destination = lax.dynamic_slice_in_dim(destination, seq_index * token_count, token_count)
    send_index = my_destination * pair_cap + local_rank
    outgoing = (
        jnp.zeros((owner_count * pair_cap, feature_width), jnp.bfloat16).at[send_index].set(merged)
    )
    incoming = lax.all_to_all(
        outgoing.reshape(owner_count, pair_cap, feature_width),
        "seq",
        split_axis=0,
        concat_axis=0,
        tiled=True,
    )
    slot_count = text_embed.shape[0]
    from_each = lax.dynamic_slice_in_dim(pair_counts, seq_index, 1, 1)[:, 0]
    offsets = jnp.cumsum(from_each) - from_each
    pair_rank = jnp.arange(pair_cap, dtype=jnp.int32)
    placement = jnp.where(
        pair_rank[None, :] < from_each[:, None], offsets[:, None] + pair_rank[None, :], slot_count
    ).reshape(-1)
    vision_slots = (
        jnp.zeros((slot_count + 1, feature_width), jnp.bfloat16)
        .at[placement]
        .set(incoming.reshape(-1, feature_width))[:slot_count]
    )
    is_vision = jnp.arange(slot_count, dtype=jnp.int32) < jnp.sum(from_each)
    filled = jnp.where(is_vision[:, None], vision_slots, text_embed)
    full_rows = lax.all_gather(filled, "tp", axis=1, tiled=True)
    lang_normed = rms_scaled(full_rows.astype(jnp.float32), lang_gain)
    lang_query = jnp.dot(lang_normed, l_query, preferred_element_type=jnp.float32).astype(
        jnp.bfloat16
    )
    lang_key = jnp.dot(lang_normed, l_key, preferred_element_type=jnp.float32).astype(jnp.bfloat16)
    lang_value = jnp.dot(lang_normed, l_value, preferred_element_type=jnp.float32).astype(
        jnp.bfloat16
    )
    kv_heads = l_key.shape[1] // LHD
    group_size = l_query.shape[1] // LHD // kv_heads
    query_five = lang_query.reshape(slot_count, kv_heads, group_size, LHD)
    key_three = lang_key.reshape(slot_count, kv_heads, LHD)
    value_three = lang_value.reshape(slot_count, kv_heads, LHD)
    position = jnp.arange(slot_count, dtype=jnp.int32)
    allowed_lang = (segment_ids[:, None] == segment_ids[None, :]) & (
        position[None, :] <= position[:, None]
    )
    scores = jnp.einsum(
        "qkgd,nkd->kgqn", query_five, key_three, preferred_element_type=jnp.float32
    ) / math.sqrt(LHD)
    scores = jnp.where(allowed_lang[None, None], scores, NEG_FILL)
    highest = jnp.max(scores, axis=-1, keepdims=True)
    weights_raw = jnp.where(allowed_lang[None, None], jnp.exp(scores - highest), 0.0)
    totals = jnp.sum(weights_raw, axis=-1)
    mixed = jnp.einsum(
        "kgqn,nkd->qkgd",
        weights_raw.astype(jnp.bfloat16),
        value_three,
        preferred_element_type=jnp.float32,
    )
    mixed = mixed / jnp.transpose(totals, (2, 0, 1))[..., None]
    lang_attended = mixed.reshape(slot_count, -1).astype(jnp.bfloat16)
    out_terms = jnp.dot(lang_attended, l_out, preferred_element_type=jnp.float32)
    summed_out = lax.psum_scatter(
        out_terms.astype(jnp.bfloat16), "tp", scatter_dimension=1, tiled=True
    ).astype(jnp.float32)
    return (filled.astype(jnp.float32) + summed_out).astype(jnp.bfloat16)


def solution(mesh):
    in_specs = (
        P("seq", None),
        P(),
        P(),
        P(None, "tp"),
        P(None, "tp"),
        P(None, "tp"),
        P("tp", None),
        P(),
        P("seq", "tp"),
        P("tp", "seq"),
        P(),
        P("seq", "tp"),
        P("seq"),
        P(),
        P(None, "tp"),
        P(None, "tp"),
        P(None, "tp"),
        P("tp", None),
    )
    out_specs = P("seq", "tp")
    return jax.shard_map(body, mesh=mesh, in_specs=in_specs, out_specs=out_specs, check_vma=False)
```

profile of v0, /device:TPU:0, one launch (start us, length us, event | category | flops | bytes accessed | tf_op | source)
XLA Modules:
  0.0 531.2 jit_solution(370896624610643545)
XLA Ops:
  7.4 1.8 fusion.11
  9.2 2.3 convolution_convert_fusion.5
  11.5 1.9 convolution_convert_fusion.6
  13.4 0.9 pad_maximum_fusion.1
  14.3 3.2 collective-permute-start
  17.5 1.3 collective-permute-start.1
  18.8 1.5 convolution_convert_fusion.4
  20.3 0.2 broadcast_in_dim.88
  20.5 0.3 reshape.206
  20.7 0.1 dynamic_slice.18
  20.8 0.1 pad_dynamic-slice_fusion
  20.9 1.4 broadcast_compare_fusion
  22.3 0.8 collective-permute-done.1
  23.1 1.4 pad_maximum_fusion
  24.5 1.1 fusion.133
  25.6 9.7 %fusion.134 = (f32[4,512]{1,0:T(4,128)S(1)}, bf16[4,512,1536]{2,1,0:T(8,128)(2,1)}) fusion(pred[512,1536]{1,0:T(8,128)(4,1)} %broadcast_compare_fusion, bf16[512,4,80]{0,2,1:T(8,128)(2,1)S(1)} %bitcast.87, bf16[1536,4,80]{0,2,1:T(8,128)(2,1)} %bitcast.82), kind=kOutput, calls=%fused_computation.167 | convolution fusion | flops 522192384 | bytes 8396800 | tf_op jit(solution)/shard_map/sub | solution.py:46
  35.3 4.8 fusion.25
  40.1 1.9 convolution_convert_fusion.2
  42.1 0.0 all-reduce.3.cloned.1.call-update
  42.1 0.0 all-gather.4.cloned.1.call-start
  42.1 0.5 all-gather.4.cloned.1.call-update
  42.7 0.0 all-gather.6.cloned.1.call-start
  42.7 0.5 all-gather.6.cloned.1.call-update
  43.3 0.2 reduce-scatter.3.cloned.1.call-start
  43.5 71.4 %all-reduce.3.cloned.1.call-done = bf16[512,1280]{1,0:T(8,128)(2,1)} async-done(((bf16[512,1280]{1,0:T(8,128)(2,1)}), bf16[512,1280]{1,0:T(8,128)(2,1)}) %all-reduce.3.cloned.1.call-update) | async-done | bytes 1310736 | tf_op jit(solution)/shard_map/psum | solution.py:101
  114.9 1.9 multiply_reduce_fusion
  116.8 0.5 multiply_convert_fusion
  117.3 0.8 reshape.209
  118.2 13.0 %all-gather.4.cloned.1.call-done = bf16[5120,1280]{1,0:T(8,128)(2,1)} async-done(((bf16[640,1280]{1,0:T(8,128)(2,1)}), bf16[5120,1280]{1,0:T(8,128)(2,1)}) %all-gather.4.cloned.1.call-update) | async-done | bytes 13107216 | tf_op jit(solution)/shard_map/all_gather | solution.py:107
  131.2 109.2 %all-gather.6.cloned.1.call-done = bf16[1280,8192]{1,0:T(8,128)(2,1)} async-done(((bf16[1280,1024]{1,0:T(8,128)(2,1)}), bf16[1280,8192]{1,0:T(8,128)(2,1)}) %all-gather.6.cloned.1.call-update) | async-done | bytes 20971536 | tf_op jit(solution)/shard_map/all_gather | solution.py:113
  240.4 19.0 %convolution_convert_fusion.1 = bf16[128,8192]{1,0:T(8,128)(2,1)} fusion(bf16[1280,8192]{1,0:T(8,128)(2,1)} %all-gather.6.cloned.1.call-done, bf16[128,5120]{1,0:T(8,128)(2,1)S(1)} %reshape.209, bf16[5120,1280]{1,0:T(8,128)(2,1)} %all-gather.4.cloned.1.call-done), kind=kOutput, calls=%fused_computation.9 | convolution fusion | flops 4373774336 | bytes 37486592 | tf_op jit(solution)/shard_map/dot_general | solution.py:111
  259.4 0.0 reduce-scatter.3.cloned.1.call-update
  259.5 0.2 fusion.48
  259.7 0.2 reduce_window_sum.18
  259.9 0.1 fusion.86
  260.0 43.5 %reduce-scatter.3.cloned.1.call-done = bf16[128,2048]{1,0:T(8,128)(2,1)} async-done(((bf16[128,8192]{1,0:T(8,128)(2,1)}), bf16[128,2048]{1,0:T(8,128)(2,1)}) %reduce-scatter.3.cloned.1.call-update) | async-done | bytes 524304 | tf_op jit(solution)/shard_map/reduce_scatter | solution.py:116
  303.5 2.9 scatter_custom_fusion
  306.4 3.7 all-to-all-start
  310.1 0.0 all-gather.8.cloned.1.call-start
  310.1 0.2 fusion.81
  310.3 0.1 constant_dynamic-slice_fusion.1
  310.4 0.8 fusion.132
  311.3 0.1 add_select_fusion
  311.3 0.1 select_n.62
  311.4 0.7 iota_compare_fusion.3
  312.1 13.4 %all-to-all-done = bf16[8,32,2048]{2,1,0:T(8,128)(2,1)S(1)} async-done(((bf16[8,32,2048]{2,1,0:T(8,128)(2,1)}), bf16[8,32,2048]{2,1,0:T(8,128)(2,1)S(1)}, u32[]{:S(2)}, u32[]{:S(2)}) %all-to-all-start) | async-done | bytes 1048608 | tf_op jit(solution)/shard_map/all_to_all | solution.py:134
  325.5 1.0 copy-done.7
  326.5 3.1 scatter_custom_fusion.1
  329.6 1.1 slice_select_fusion
  330.7 0.0 all-gather.8.cloned.1.call-update
  330.7 0.3 reduce-scatter.5.cloned.1.call-start
  331.0 0.1 fusion.80
  331.1 78.1 %all-gather.8.cloned.1.call-done = bf16[256,8192]{1,0:T(8,128)(2,1)} async-done(((bf16[256,2048]{1,0:T(8,128)(2,1)}), bf16[256,8192]{1,0:T(8,128)(2,1)}) %all-gather.8.cloned.1.call-update) | async-done | bytes 4194320 | tf_op jit(solution)/shard_map/all_gather | solution.py:155
  409.2 3.3 fusion.3
  412.5 0.2 copy-done.5
  412.7 8.2 %convolution_convert_fusion.3 = bf16[256,1024]{1,0:T(8,128)(2,1)S(1)} fusion(bf16[8192,1024]{1,0:T(8,128)(2,1)} %param.32, bf16[256,8192]{1,0:T(8,128)(2,1)S(1)} %copy-done.5, f32[8192]{0:T(1024)S(1)} %copy-done.13, f32[256]{0:T(256)S(1)} %add_rsqrt_fusion.2), kind=kOutput, calls=%fused_computation.38 | convolution fusion | flops 4303618048 | bytes 21529600 | tf_op jit(solution)/shard_map/dot_general | solution.py:157
  420.9 0.4 reshape.214
  421.3 5.6 %convolution_convert_fusion.7 = bf16[256,256]{0,1:T(8,128)(2,1)S(1)} fusion(bf16[8192,256]{1,0:T(8,128)(2,1)} %param.33, bf16[256,8192]{1,0:T(8,128)(2,1)} %all-gather.8.cloned.1.call-done, f32[8192]{0:T(1024)S(1)} %copy-done.13, f32[256]{0:T(256)S(1)} %add_rsqrt_fusion.2), kind=kOutput, calls=%fused_computation.45 | convolution fusion | flops 1082195968 | bytes 8553472 | tf_op jit(solution)/shard_map/dot_general | solution.py:160
  426.9 1.1 fusion.135
  428.0 5.6 %convolution_convert_fusion.8 = bf16[256,256]{0,1:T(8,128)(2,1)S(1)} fusion(bf16[8192,256]{1,0:T(8,128)(2,1)} %param.34, bf16[256,8192]{1,0:T(8,128)(2,1)} %all-gather.8.cloned.1.call-done, f32[8192]{0:T(1024)S(1)} %copy-done.13, f32[256]{0:T(256)S(1)} %add_rsqrt_fusion.2), kind=kOutput, calls=%fused_computation.46 | convolution fusion | flops 1082195968 | bytes 8553472 | tf_op jit(solution)/shard_map/dot_general | solution.py:161
  433.6 0.3 fusion.18
  433.9 12.0 %convolution_convert_fusion = bf16[256,8192]{1,0:T(8,128)(2,1)} fusion(bf16[256,1024]{0,1:T(8,128)(2,1)S(1)} %bitcast.83, bf16[1024,8192]{1,0:T(8,128)(2,1)} %param.35), kind=kOutput, calls=%fused_computation.8 | convolution fusion | flops 4297064448 | bytes 21495808 | tf_op jit(solution)/shard_map/dot_general | solution.py:188
  446.0 75.4 %reduce-scatter.5.cloned.1.call-done = bf16[256,2048]{1,0:T(8,128)(2,1)} async-done(((bf16[256,8192]{1,0:T(8,128)(2,1)}), bf16[256,2048]{1,0:T(8,128)(2,1)}) %reduce-scatter.5.cloned.1.call-update) | async-done | bytes 1048592 | tf_op jit(solution)/shard_map/reduce_scatter | solution.py:189
  521.5 2.6 add_convert_fusion
  (40 shorter events, 0.2 us)
Async XLA Ops:
  7.4 32.8 %copy-start = (bf16[320,1280]{1,0:T(8,128)(2,1)S(1)}, bf16[320,1280]{1,0:T(8,128)(2,1)}, u32[]{:S(2)}) copy-start(bf16[320,1280]{1,0:T(8,128)(2,1)} %param.24) | copy-start | bytes 2457604
  7.4 4.1 copy-start.2
  7.4 4.1 copy-start.14
  7.4 107.5 %all-reduce.3.cloned.1.call-start = ((), (), s32[]{:S(2)}) async-start(), calls=%async_computation.3 | async-start | bytes 2621440 | tf_op jit(solution)/shard_map/psum | solution.py:101
  11.5 7.3 %copy-start.12 = (bf16[1280,320]{0,1:T(8,128)(2,1)S(1)}, bf16[1280,320]{0,1:T(8,128)(2,1)}, u32[]{:S(2)}) copy-start(bf16[1280,320]{0,1:T(8,128)(2,1)} %param.21) | copy-start | bytes 2457604
  13.4 6.9 %copy-start.10 = (s32[1024]{0:T(1024)S(1)}, s32[1024]{0:T(1024)}, u32[]{:S(2)}) copy-start(s32[1024]{0:T(1024)} %param.19) | copy-start | bytes 12292
  14.3 8.0 %collective-permute-start = (bf16[512,640]{0,1:T(8,128)(2,1)}, bf16[512,640]{0,1:T(8,128)(2,1)}, u32[]{:S(2)}, u32[]{:S(2)}) collective-permute-start(bf16[512,640]{0,1:T(8,128)(2,1)} %pad_maximum_fusion.1), channel_id=1, source_target_pairs={{0,4},{4,8},{8,12},{12,16},{16,20},{20,24},{24,28},{1,5},{5,9},{9,... | collective-permute-start | bytes 1966088 | tf_op jit(solution)/shard_map/ppermute | solution.py:25
  17.5 5.6 %collective-permute-start.1 = (bf16[512,640]{0,1:T(8,128)(2,1)}, bf16[512,640]{0,1:T(8,128)(2,1)}, u32[]{:S(2)}, u32[]{:S(2)}) collective-permute-start(bf16[512,640]{0,1:T(8,128)(2,1)} %pad_maximum_fusion.1), channel_id=1, source_target_pairs={{4,0},{8,4},{12,8},{16,12},{20,16},{24,20},{28,24},{5,1},{9,5},{13... | collective-permute-start | bytes 1966088 | tf_op jit(solution)/shard_map/ppermute | solution.py:27
  24.5 1.1 copy-start.15
  42.1 89.1 %all-gather.4.cloned.1.call-start = ((), (), s32[]{:S(2)}) async-start(), calls=%async_computation.4 | async-start | bytes 14745600 | tf_op jit(solution)/shard_map/all_gather | solution.py:107
  42.7 74.1 %copy-start.9 = (f32[1280]{0:T(1024)S(1)}, f32[1280]{0:T(1024)}, u32[]{:S(2)}) copy-start(f32[1280]{0:T(1024)} %param.25) | copy-start | bytes 15364
  42.7 197.8 %all-gather.6.cloned.1.call-start = ((), (), s32[]{:S(2)}) async-start(), calls=%async_computation.5 | async-start | bytes 23592960 | tf_op jit(solution)/shard_map/all_gather | solution.py:113
  43.3 260.2 %reduce-scatter.3.cloned.1.call-start = ((), (), s32[]{:S(2)}) async-start(), calls=%async_computation.6 | async-start | bytes 2621440 | tf_op jit(solution)/shard_map/reduce_scatter | solution.py:116
  114.9 1.9 copy-start.4
  118.2 141.3 %copy-start.8 = (s32[1024,1]{0,1:T(1,128)S(1)}, s32[1024,1]{0,1:T(1,128)}, u32[]{:S(2)}) copy-start(s32[1024,1]{0,1:T(1,128)} %param.28) | copy-start | bytes 12292
  259.5 70.1 %copy-start.6 = (bf16[256,2048]{1,0:T(8,128)(2,1)S(1)}, bf16[256,2048]{1,0:T(8,128)(2,1)}, u32[]{:S(2)}) copy-start(bf16[256,2048]{1,0:T(8,128)(2,1)} %param.29) | copy-start | bytes 3145732
  306.4 19.1 %all-to-all-start = ((bf16[8,32,2048]{2,1,0:T(8,128)(2,1)}), bf16[8,32,2048]{2,1,0:T(8,128)(2,1)S(1)}, u32[]{:S(2)}, u32[]{:S(2)}) async-start(bf16[8,32,2048]{2,1,0:T(8,128)(2,1)} %bitcast.11), calls=%async_computation.1 | async-start | bytes 2097152 | tf_op jit(solution)/shard_map/all_to_all | solution.py:134
  310.1 99.1 %all-gather.8.cloned.1.call-start = ((), (), s32[]{:S(2)}) async-start(), calls=%async_computation.7 | async-start | bytes 5242880 | tf_op jit(solution)/shard_map/all_gather | solution.py:155
  325.5 1.0 copy-start.7
  326.5 4.6 copy-start.11
  330.7 81.8 %copy-start.13 = (f32[8192]{0:T(1024)S(1)}, f32[8192]{0:T(1024)}, u32[]{:S(2)}) copy-start(f32[8192]{0:T(1024)} %param.31) | copy-start | bytes 98308
  330.7 190.7 %reduce-scatter.5.cloned.1.call-start = ((), (), s32[]{:S(2)}) async-start(), calls=%async_computation.8 | async-start | bytes 5242880 | tf_op jit(solution)/shard_map/reduce_scatter | solution.py:189
  409.2 3.4 copy-start.5
  446.0 75.5 %copy-start.3 = (bf16[256,2048]{1,0:T(8,128)(2,1)S(1)}, bf16[256,2048]{1,0:T(8,128)(2,1)}, u32[]{:S(2)}) copy-start(bf16[256,2048]{1,0:T(8,128)(2,1)} %slice_select_fusion) | copy-start | bytes 3145732
  446.0 78.0 %copy-start.1 = (bf16[320,1280]{1,0:T(8,128)(2,1)S(1)}, bf16[320,1280]{1,0:T(8,128)(2,1)}, u32[]{:S(2)}) copy-start(bf16[320,1280]{1,0:T(8,128)(2,1)} %param.24) | copy-start | bytes 2457604
Sparse Core Ops, SparseCore 0:
  42.2 72.6 all-reduce.2
  259.6 43.8 reduce-scatter.2
  330.9 78.3 all-gather.7
  446.1 75.2 reduce-scatter.4
Sparse Core Ops, SparseCore 1:
  44.5 86.7 all-gather.3
  133.0 107.4 all-gather.5
where the time goes:
time: 532 us; the launch traced here: 531 us
  waiting for transfers between devices  406 us (76%)
  matrix products  74 us (14%)
  other arithmetic  17.3 us (3%)
  between operations  14.9 us (3%)
  local copies, waits for them, and re-layouts  10.3 us (2%)
  starting transfers between devices  8.75 us (2%)
    all_gather x1, waiting for transfers between devices, body(): lax.all_gather(merge_down, 'seq', axis=1, tiled=True)  109 us
    all_gather x1, waiting for transfers between devices, body(): full_rows = lax.all_gather(filled, 'tp', axis=1, tiled=True)  78.1 us
    reduce_scatter x1, waiting for transfers between devices, body(): lax.psum_scatter(out_terms.astype(jnp.bfloat16), 'tp', scatter_dimension=...  75.4 us
    psum x1, waiting for transfers between devices, body(): lax.psum(partial_value.astype(jnp.bfloat16), 'tp').astype(jnp.float32)  71.4 us
    reduce_scatter x1, waiting for transfers between devices, body(): lax.psum_scatter(down_terms.astype(jnp.bfloat16), 'tp', scatter_dimension...  43.5 us
    dot_general x1, matrix products, body(): jnp.dot(hidden, lax.all_gather(merge_down, 'seq', axis=1, tiled=True), pr...  19 us
    all_to_all x1, waiting for transfers between devices, body(): lax.all_to_all(outgoing.reshape(owner_count, pair_cap, feature_width), 's...  13.4 us
    all_gather x1, waiting for transfers between devices, body(): lax.all_gather(merge_up, 'seq', axis=0, tiled=True)  13 us
  transfers between devices with their start and end apart: 9, of which 8 were waited for; matrix products, arithmetic and copies ran while one was open for 2% of the time, Pallas kernels for 0%

commit v1 on v0

--- a/solution.py
+++ b/solution.py
@@ -75,16 +75,35 @@
     l_value,
     l_out,
 ):
+    seq_count, tp_count = lax.axis_size("seq"), lax.axis_size("tp")
+    seq_index, tp_index = lax.axis_index("seq"), lax.axis_index("tp")
     row_count = patches.shape[0]
     local_width = v_query.shape[1]
     head_size = DV // VHEADS
     head_count = local_width // head_size
     score_scale = 1.0 / math.sqrt(head_size)
-    seq_index = lax.axis_index("seq")
+
+    out_rows = v_out.shape[0] // seq_count
+    v_out_whole = lax.all_gather(
+        lax.dynamic_slice_in_dim(v_out, seq_index * out_rows, out_rows),
+        ("tp", "seq"),
+        axis=0,
+        tiled=True,
+    )
+    text_rows = lax.all_gather(text_embed, "tp", axis=1, tiled=True)
+    lang_rows = l_out.shape[0] // seq_count
+    l_out_cut = lax.all_to_all(
+        lax.dynamic_slice_in_dim(l_out, seq_index * lang_rows, lang_rows),
+        "tp",
+        split_axis=1,
+        concat_axis=0,
+        tiled=True,
+    )
+    l_out_columns = lax.all_gather(l_out_cut, "seq", axis=0, tiled=True)
+
     patch_ids = jnp.repeat(image_ids, 4)
     my_ids = lax.dynamic_slice_in_dim(patch_ids, seq_index * row_count, row_count)
-    vision_state = patches.astype(jnp.float32)
-    normed = rms_scaled(vision_state, vision_gain)
+    normed = rms_scaled(patches.astype(jnp.float32), vision_gain)
     query_rows = jnp.dot(normed, v_query, preferred_element_type=jnp.float32).astype(jnp.bfloat16)
     key_part = jnp.dot(normed, v_key, preferred_element_type=jnp.float32).astype(jnp.bfloat16)
     value_part = jnp.dot(normed, v_value, preferred_element_type=jnp.float32).astype(jnp.bfloat16)
@@ -97,63 +116,72 @@
     nearby_keys = nearby[:, :local_width].reshape(3 * row_count, head_count, head_size)
     nearby_values = nearby[:, local_width:].reshape(3 * row_count, head_count, head_size)
     attended = masked_attend(query_grid, nearby_keys, nearby_values, allowed, score_scale)
-    partial_value = jnp.dot(attended, v_out, preferred_element_type=jnp.float32)
-    summed = lax.psum(partial_value.astype(jnp.bfloat16), "tp").astype(jnp.float32)
-    merge_normed = rms_scaled(vision_state + summed, merge_gain)
+
+    attended = lax.all_to_all(attended, "tp", split_axis=0, concat_axis=1, tiled=True)
+    own_rows = row_count // tp_count
+    own_patches = lax.dynamic_slice_in_dim(patches, tp_index * own_rows, own_rows)
+    vision_state = own_patches.astype(jnp.float32) + jnp.dot(
+        attended, v_out_whole, preferred_element_type=jnp.float32
+    )
+    merge_rows = rms_scaled(vision_state, merge_gain).reshape(own_rows // 4, 4 * DV)
+
+    own_tokens = own_rows // 4
+    spread = lax.all_to_all(merge_rows, "seq", split_axis=1, concat_axis=0, tiled=True)
+    spread = lax.all_gather(spread, "tp", axis=0, tiled=True)
+    spread = jnp.swapaxes(spread.reshape(tp_count, seq_count, own_tokens, -1), 0, 1)
+    spread = spread.reshape(tp_count * seq_count * own_tokens, -1)
+    up_terms = jnp.dot(spread, merge_up, preferred_element_type=jnp.float32)
+    hidden_sum = lax.psum_scatter(
+        up_terms.astype(jnp.bfloat16), "seq", scatter_dimension=0, tiled=True
+    ).astype(jnp.float32)
+    hidden = jax.nn.gelu(hidden_sum, approximate=False).astype(jnp.bfloat16)
+    hidden = lax.all_gather(hidden, "seq", axis=0, tiled=True)
+    down_terms = jnp.dot(hidden, merge_down, preferred_element_type=jnp.float32)
+    merged = lax.psum_scatter(
+        down_terms.astype(jnp.bfloat16), "tp", scatter_dimension=0, tiled=True
+    )
+
     token_count = row_count // 4
-    merge_rows = merge_normed.reshape(token_count, 4 * DV)
-    hidden_sum = jnp.dot(
-        merge_rows,
-        lax.all_gather(merge_up, "seq", axis=0, tiled=True),
-        preferred_element_type=jnp.float32,
-    )
-    hidden = jax.nn.gelu(hidden_sum, approximate=False).astype(jnp.bfloat16)
-    down_terms = jnp.dot(
-        hidden,
-        lax.all_gather(merge_down, "seq", axis=1, tiled=True),
-        preferred_element_type=jnp.float32,
-    )
-    merged = lax.psum_scatter(
-        down_terms.astype(jnp.bfloat16), "tp", scatter_dimension=1, tiled=True
-    )
-    owner_count = lax.axis_size("seq")
-    pair_cap = 2 * token_count // owner_count
-    feature_width = merged.shape[1]
-    owner_iota = jnp.arange(owner_count, dtype=jnp.int32)
+    all_tokens = token_count * seq_count
+    group = all_tokens // tp_count
+    cap = (2 * token_count // seq_count) * (group // token_count)
     destination = owners[:, 0]
-    one_hot = (destination[:, None] == owner_iota[None, :]).astype(jnp.int32)
-    grid_counts = one_hot.reshape(owner_count, token_count, owner_count)
-    pair_counts = jnp.sum(grid_counts, axis=1)
-    mine = lax.dynamic_slice_in_dim(grid_counts, seq_index, 1, 0)[0]
-    local_rank = jnp.sum((jnp.cumsum(mine, axis=0) - mine) * mine, axis=1)
-    my_destination = lax.dynamic_slice_in_dim(destination, seq_index * token_count, token_count)
-    send_index = my_destination * pair_cap + local_rank
-    outgoing = (
-        jnp.zeros((owner_count * pair_cap, feature_width), jnp.bfloat16).at[send_index].set(merged)
-    )
+    one_hot = (
+        destination[:, None] == jnp.arange(seq_count, dtype=jnp.int32)[None, :]
+    ).astype(jnp.int32)
+    grid_counts = one_hot.reshape(tp_count, group, seq_count)
+    mine = lax.dynamic_slice_in_dim(grid_counts, tp_index, 1, 0)[0]
+    rank = jnp.sum((jnp.cumsum(mine, axis=0) - mine) * mine, axis=1)
+    send_index = lax.dynamic_slice_in_dim(destination, tp_index * group, group) * cap + rank
+    send_place = jnp.arange(seq_count * cap, dtype=jnp.int32)[:, None] == send_index[None, :]
+    outgoing = jnp.dot(
+        send_place.astype(jnp.bfloat16), merged, preferred_element_type=jnp.float32
+    ).astype(jnp.bfloat16)
     incoming = lax.all_to_all(
-        outgoing.reshape(owner_count, pair_cap, feature_width),
-        "seq",
-        split_axis=0,
-        concat_axis=0,
-        tiled=True,
-    )
+        outgoing.reshape(seq_count, cap, -1), "seq", split_axis=0, concat_axis=2, tiled=True
+    )[0]
+    arrived = lax.all_gather(incoming, "tp", axis=0, tiled=True)
     slot_count = text_embed.shape[0]
-    from_each = lax.dynamic_slice_in_dim(pair_counts, seq_index, 1, 1)[:, 0]
+    group_counts = jnp.sum(grid_counts, axis=1)
+    from_each = lax.dynamic_slice_in_dim(group_counts, seq_index, 1, 1)[:, 0]
     offsets = jnp.cumsum(from_each) - from_each
-    pair_rank = jnp.arange(pair_cap, dtype=jnp.int32)
-    placement = jnp.where(
-        pair_rank[None, :] < from_each[:, None], offsets[:, None] + pair_rank[None, :], slot_count
+    cap_rank = jnp.arange(cap, dtype=jnp.int32)
+    slot_of = jnp.where(
+        cap_rank[None, :] < from_each[:, None], offsets[:, None] + cap_rank[None, :], slot_count
     ).reshape(-1)
-    vision_slots = (
-        jnp.zeros((slot_count + 1, feature_width), jnp.bfloat16)
-        .at[placement]
-        .set(incoming.reshape(-1, feature_width))[:slot_count]
-    )
-    is_vision = jnp.arange(slot_count, dtype=jnp.int32) < jnp.sum(from_each)
-    filled = jnp.where(is_vision[:, None], vision_slots, text_embed)
-    full_rows = lax.all_gather(filled, "tp", axis=1, tiled=True)
-    lang_normed = rms_scaled(full_rows.astype(jnp.float32), lang_gain)
+    slots = jnp.arange(slot_count, dtype=jnp.int32)
+    slot_place = slots[:, None] == slot_of[None, :]
+    vision_slots = jnp.dot(
+        slot_place.astype(jnp.bfloat16), arrived, preferred_element_type=jnp.float32
+    ).astype(jnp.bfloat16)
+    is_vision = slots < jnp.sum(from_each)
+    full_rows = jnp.where(is_vision[:, None], vision_slots, text_rows)
+    own_width = text_embed.shape[1]
+    filled = lax.dynamic_slice_in_dim(full_rows, tp_index * own_width, own_width, axis=1)
+
+    lang_normed = lax.optimization_barrier(
+        rms_scaled(full_rows.astype(jnp.float32), lang_gain)
+    )
     lang_query = jnp.dot(lang_normed, l_query, preferred_element_type=jnp.float32).astype(
         jnp.bfloat16
     )
@@ -166,9 +194,8 @@
     query_five = lang_query.reshape(slot_count, kv_heads, group_size, LHD)
     key_three = lang_key.reshape(slot_count, kv_heads, LHD)
     value_three = lang_value.reshape(slot_count, kv_heads, LHD)
-    position = jnp.arange(slot_count, dtype=jnp.int32)
     allowed_lang = (segment_ids[:, None] == segment_ids[None, :]) & (
-        position[None, :] <= position[:, None]
+        slots[None, :] <= slots[:, None]
     )
     scores = jnp.einsum(
         "qkgd,nkd->kgqn", query_five, key_three, preferred_element_type=jnp.float32
@@ -185,10 +212,10 @@
     )
     mixed = mixed / jnp.transpose(totals, (2, 0, 1))[..., None]
     lang_attended = mixed.reshape(slot_count, -1).astype(jnp.bfloat16)
-    out_terms = jnp.dot(lang_attended, l_out, preferred_element_type=jnp.float32)
-    summed_out = lax.psum_scatter(
-        out_terms.astype(jnp.bfloat16), "tp", scatter_dimension=1, tiled=True
-    ).astype(jnp.float32)
+    heads = lax.all_gather(lang_attended, "tp", axis=0)
+    heads = heads.reshape(tp_count, slot_count, seq_count, lang_rows)
+    heads = jnp.transpose(heads, (1, 2, 0, 3)).reshape(slot_count, -1)
+    summed_out = jnp.dot(heads, l_out_columns, preferred_element_type=jnp.float32)
     return (filled.astype(jnp.float32) + summed_out).astype(jnp.bfloat16)
 
 

time: 532 us -> 644 us (1.21)
  waiting for transfers between devices: 406 us -> 476 us
  blocking collectives: 0 us -> 31.8 us
  local copies, waits for them, and re-layouts: 10.3 us -> 25.2 us
    all_gather x3 -> x7, waiting for transfers between devices: 200 us -> 384 us  [the longest x1 94.9 us: body(): text_rows = lax.all_gather(text_embed, 'tp', axis=1, tiled=True)]
    psum x1 -> x0, waiting for transfers between devices: 71.4 us -> none  [body(): lax.psum(partial_value.astype(jnp.bfloat16), 'tp').astype(jnp.float32)]
    reduce_scatter x1, waiting for transfers between devices: 75.4 us -> 42.6 us  [body(): lax.psum_scatter(up_terms.astype(jnp.bfloat16), 'seq', scatter_dimension=...]
    all_to_all x0 -> x2, blocking collectives: none -> 31.8 us  [the longest x1 18.8 us: body(): lax.all_to_all(outgoing.reshape(seq_count, cap, -1), 'seq', split_axis=0,...]
    unnamed x32 -> x39, local copies, waits for them, and re-layouts: 1.22 us -> 8.29 us
    all_to_all x1 -> x2, waiting for transfers between devices: 13.4 us -> 7.3 us  [the longest x1 7.3 us: body(): lax.all_to_all(attended, 'tp', split_axis=0, concat_axis=1, tiled=True)]
    dot_general x3 -> x6, matrix products: 33 us -> 31.1 us  [the longest x1 12.2 us: body(): jnp.dot(heads, l_out_columns, preferred_element_type=jnp.float32)]
  transfers between devices with their start and end apart: 9 -> 13, of which waited for: 8 -> 11; matrix products, arithmetic and copies ran while one was open for 2% -> 11% of each run, Pallas kernels for 0% -> 0%
where the time goes in v1:
time: 644 us; the launch traced here: 643 us
  waiting for transfers between devices  476 us (74%)
  matrix products  69 us (11%)
  blocking collectives  31.8 us (5%)
  local copies, waits for them, and re-layouts  25.2 us (4%)
  starting transfers between devices  14 us (2%)
  between operations  13.6 us (2%)
  other arithmetic  13 us (2%)
    all_gather x1, waiting for transfers between devices, body(): text_rows = lax.all_gather(text_embed, 'tp', axis=1, tiled=True)  94.9 us
    all_gather x1, waiting for transfers between devices, body(): l_out_columns = lax.all_gather(l_out_cut, 'seq', axis=0, tiled=True)  86.3 us
    all_gather x1, waiting for transfers between devices, body(): arrived = lax.all_gather(incoming, 'tp', axis=0, tiled=True)  80.8 us
    reduce_scatter x1, waiting for transfers between devices, body(): lax.psum_scatter(up_terms.astype(jnp.bfloat16), 'seq', scatter_dimension=...  42.6 us
    all_gather x1, waiting for transfers between devices, body(): heads = lax.all_gather(lang_attended, 'tp', axis=0)  41.6 us
    reduce_scatter x1, waiting for transfers between devices, body(): lax.psum_scatter(down_terms.astype(jnp.bfloat16), 'tp', scatter_dimension...  41.2 us
    all_gather x1, waiting for transfers between devices, body(): spread = lax.all_gather(spread, 'tp', axis=0, tiled=True)  30.3 us
    all_gather x1, waiting for transfers between devices, body(): hidden = lax.all_gather(hidden, 'seq', axis=0, tiled=True)  30.2 us
  transfers between devices with their start and end apart: 13, of which 11 were waited for; matrix products, arithmetic and copies ran while one was open for 11% of the time, Pallas kernels for 0%

profile of v1, /device:TPU:0, one launch (start us, length us, event | category | flops | bytes accessed | tf_op | source)
XLA Modules:
  0.0 642.9 jit_solution(11493029618187922925)
XLA Ops:
  6.5 1.7 constant_dynamic-slice_fusion.1
  8.3 1.8 fusion.12
  10.1 2.3 convolution_convert_fusion.6
  12.4 0.7 convolution_convert_fusion.7
  13.2 0.7 copy-done.7
  13.9 0.9 pad_maximum_fusion.1
  14.8 3.2 collective-permute-start
  18.0 1.3 collective-permute-start.1
  19.3 1.5 convolution_convert_fusion.5
  20.9 0.3 reshape.232
  21.4 1.4 broadcast_compare_fusion
  22.8 0.8 collective-permute-done.1
  23.6 1.5 pad_maximum_fusion
  25.1 1.4 fusion.88
  26.5 9.2 %fusion.89 = (f32[4,512]{1,0:T(4,128)S(1)}, bf16[4,512,1536]{2,1,0:T(8,128)(2,1)}) fusion(pred[512,1536]{1,0:T(8,128)(4,1)S(1)} %copy-done.8, bf16[512,4,80]{0,2,1:T(8,128)(2,1)} %bitcast.122, bf16[1536,4,80]{0,2,1:T(8,128)(2,1)} %bitcast.117), kind=kOutput, calls=%fused_computation.121 | convolution fusion | flops 522192384 | bytes 8396800 | tf_op jit(solution)/shard_map/sub | solution.py:46
  35.7 5.2 fusion.27
  41.0 0.8 copy.51
  41.8 5.0 all-to-all-start
  46.8 7.3 %all-to-all-done = bf16[4,128,320]{1,2,0:T(8,128)(2,1)S(1)} async-done(((bf16[4,128,320]{1,2,0:T(8,128)(2,1)}), bf16[4,128,320]{1,2,0:T(8,128)(2,1)S(1)}, u32[]{:S(2)}, u32[]{:S(2)}) %all-to-all-start) | async-done | bytes 327712 | tf_op jit(solution)/shard_map/all_to_all | solution.py:120
  54.1 19.6 %all-gather.8.cloned.1.call-done = bf16[1280,1280]{1,0:T(8,128)(2,1)} async-done(((bf16[40,1280]{1,0:T(8,128)(2,1)}), bf16[1280,1280]{1,0:T(8,128)(2,1)}) %all-gather.8.cloned.1.call-update) | async-done | bytes 3276816 | tf_op jit(solution)/shard_map/all_gather | solution.py:87
  73.7 2.7 multiply_reduce_fusion
  76.7 13.0 %all_to_all.69 = bf16[32,8,640]{2,0,1:T(8,128)(2,1)} all-to-all(bf16[32,8,640]{2,0,1:T(8,128)(2,1)S(1)} %copy.52), channel_id=1, replica_groups=mesh['seq'=8,'tp'=4] {'seq'}, dimensions={1} | all-to-all | bytes 655360 | tf_op jit(solution)/shard_map/all_to_all | solution.py:129
  89.8 30.3 %all-gather.10.cloned.1.call-done = bf16[1024,640]{1,0:T(8,128)(2,1)} async-done(((bf16[256,640]{1,0:T(8,128)(2,1)}), bf16[1024,640]{1,0:T(8,128)(2,1)}) %all-gather.10.cloned.1.call-update) | async-done | bytes 1310736 | tf_op jit(solution)/shard_map/all_gather | solution.py:130
  120.1 1.6 copy.53
  121.9 3.7 convolution_convert_fusion.1
  125.7 0.2 all-gather.12.cloned.1.call-start
  125.9 42.6 %reduce-scatter.3.cloned.1.call-done = bf16[128,1280]{1,0:T(8,128)(2,1)} async-done(((bf16[1024,1280]{1,0:T(8,128)(2,1)}), bf16[128,1280]{1,0:T(8,128)(2,1)}) %reduce-scatter.3.cloned.1.call-update) | async-done | bytes 327696 | tf_op jit(solution)/shard_map/reduce_scatter | solution.py:134
  168.5 3.1 fusion.35
  171.7 30.2 %all-gather.12.cloned.1.call-done = bf16[1024,1280]{1,0:T(8,128)(2,1)} async-done(((bf16[128,1280]{1,0:T(8,128)(2,1)}), bf16[1024,1280]{1,0:T(8,128)(2,1)}) %all-gather.12.cloned.1.call-update) | async-done | bytes 2621456 | tf_op jit(solution)/shard_map/all_gather | solution.py:138
  201.9 5.9 convolution_convert_fusion.2
  207.8 0.5 all-gather.16.cloned.1.call-update
  208.4 0.5 broadcast.134
  208.9 0.7 reduce.9
  209.6 0.6 reduce-window.11
  210.6 41.2 %reduce-scatter.5.cloned.1.call-done = bf16[256,1024]{1,0:T(8,128)(2,1)} async-done(((bf16[1024,1024]{1,0:T(8,128)(2,1)}), bf16[256,1024]{1,0:T(8,128)(2,1)}) %reduce-scatter.5.cloned.1.call-update) | async-done | bytes 524304 | tf_op jit(solution)/shard_map/reduce_scatter | solution.py:140
  251.8 1.5 convolution_convert_fusion.3
  253.3 18.8 %all_to_all.70 = bf16[8,64,1024]{2,1,0:T(8,128)(2,1)S(1)} all-to-all(bf16[8,64,1024]{2,1,0:T(8,128)(2,1)S(1)} %bitcast.110), channel_id=1, replica_groups=mesh['seq'=8,'tp'=4] {'seq'}, dimensions={0} | all-to-all | bytes 2097152 | tf_op jit(solution)/shard_map/all_to_all | solution.py:160
  272.1 1.1 copy.69
  273.2 1.8 constant_dynamic-slice_fusion
  275.0 2.5 copy.68
  277.5 3.7 all-to-all-start.3
  281.5 0.7 fusion.87
  282.4 0.6 iota_compare_fusion.7
  283.1 94.9 %all-gather.16.cloned.1.call-done = bf16[256,8192]{1,0:T(8,128)(2,1)} async-done(((bf16[256,2048]{1,0:T(8,128)(2,1)}), bf16[256,8192]{1,0:T(8,128)(2,1)}) %all-gather.16.cloned.1.call-update) | async-done | bytes 4194320 | tf_op jit(solution)/shard_map/all_gather | solution.py:93
  378.0 80.8 %all-gather.14.cloned.1.call-done = bf16[256,8192]{1,0:T(8,128)(2,1)} async-done(((bf16[64,8192]{1,0:T(8,128)(2,1)}), bf16[256,8192]{1,0:T(8,128)(2,1)}) %all-gather.14.cloned.1.call-update) | async-done | bytes 4194320 | tf_op jit(solution)/shard_map/all_gather | solution.py:163
  458.8 5.1 fusion.4
  464.0 1.2 fusion.6
  465.2 0.7 copy-done.4
  465.9 1.9 copy-done.2
  467.9 8.2 %convolution_convert_fusion.4 = bf16[256,1024]{1,0:T(8,128)(2,1)S(1)} fusion(bf16[256,8192]{1,0:T(8,128)(2,1)S(1)} %fusion.6, bf16[8192,1024]{1,0:T(8,128)(2,1)} %param.32), kind=kOutput, calls=%fused_computation.37 | convolution fusion | flops 4295229440 | bytes 21495808 | tf_op jit(solution)/shard_map/dot_general | solution.py:185
  476.1 0.4 reshape.240
  476.5 5.3 convolution_convert_fusion.8
  481.8 0.6 copy-done.5
  482.4 1.8 convolution_convert_fusion.9
  484.2 2.0 fusion.90
  486.3 1.5 fusion.20
  487.8 1.0 copy.58
  488.8 0.3 all-gather.20.cloned.1.call-start
  489.1 2.7 copy.62
  491.9 41.6 %all-gather.18.cloned.1.call-done = bf16[4,256,1024]{2,1,0:T(8,128)(2,1)} async-done(((bf16[1,256,1024]{2,1,0:T(8,128)(2,1)}), bf16[4,256,1024]{2,1,0:T(8,128)(2,1)}) %all-gather.18.cloned.1.call-update) | async-done | bytes 2097168 | tf_op jit(solution)/shard_map/all_gather | solution.py:215
  533.5 2.8 copy.59
  536.3 1.5 copy.60
  537.9 86.3 %all-gather.20.cloned.1.call-done = bf16[4096,2048]{1,0:T(8,128)(2,1)} async-done(((bf16[512,2048]{1,0:T(8,128)(2,1)}), bf16[4096,2048]{1,0:T(8,128)(2,1)}) %all-gather.20.cloned.1.call-update) | async-done | bytes 16777232 | tf_op jit(solution)/shard_map/all_gather | solution.py:102
  624.1 12.2 %fusion.15 = bf16[256,2048]{1,0:T(8,128)(2,1)} fusion(bf16[256,4096]{0,1:T(8,128)(2,1)} %bitcast.104, bf16[4096,2048]{1,0:T(8,128)(2,1)} %all-gather.20.cloned.1.call-done, bf16[256,8192]{1,0:T(8,128)(2,1)} %copy-done.4, s32[]{:T(128)S(6)} %select_n.68), kind=kOutput, calls=%fused_computation.24 | convolution fusion | flops 4296540160 | bytes 20971524 | tf_op jit(solution)/shard_map/dot_general | solution.py:218
  (74 shorter events, 2.3 us)
Async XLA Ops:
  6.5 195.3 %copy-start = (bf16[1280,1024]{1,0:T(8,128)(2,1)S(1)}, bf16[1280,1024]{1,0:T(8,128)(2,1)}, u32[]{:S(2)}) copy-start(bf16[1280,1024]{1,0:T(8,128)(2,1)} %param.27) | copy-start | bytes 7864324
  6.5 67.2 %all-gather.8.cloned.1.call-start = ((), (), s32[]{:S(2)}) async-start(), calls=%async_computation.6 | async-start | bytes 3379200 | tf_op jit(solution)/shard_map/all_gather | solution.py:87
  8.3 4.1 copy-start.6
  8.3 4.1 copy-start.15
  8.3 4.1 copy-start.17
  12.4 6.9 %copy-start.16 = (bf16[1280,320]{0,1:T(8,128)(2,1)S(1)}, bf16[1280,320]{0,1:T(8,128)(2,1)}, u32[]{:S(2)}) copy-start(bf16[1280,320]{0,1:T(8,128)(2,1)} %param.21) | copy-start | bytes 2457604
  13.1 0.7 copy-start.7
  13.9 6.9 %copy-start.12 = (s32[1024]{0:T(1024)S(1)}, s32[1024]{0:T(1024)}, u32[]{:S(2)}) copy-start(s32[1024]{0:T(1024)} %param.19) | copy-start | bytes 12292
  14.8 8.0 %collective-permute-start = (bf16[512,640]{0,1:T(8,128)(2,1)}, bf16[512,640]{0,1:T(8,128)(2,1)}, u32[]{:S(2)}, u32[]{:S(2)}) collective-permute-start(bf16[512,640]{0,1:T(8,128)(2,1)} %pad_maximum_fusion.1), channel_id=1, source_target_pairs={{0,4},{4,8},{8,12},{12,16},{16,20},{20,24},{24,28},{1,5},{5,9},{9,... | collective-permute-start | bytes 1966088 | tf_op jit(solution)/shard_map/ppermute | solution.py:25
  18.0 5.6 collective-permute-start.1
  25.1 1.4 copy-start.8
  41.8 34.7 %copy-start.10 = (f32[1280]{0:T(1024)S(1)}, f32[1280]{0:T(1024)}, u32[]{:S(2)}) copy-start(f32[1280]{0:T(1024)} %param.25) | copy-start | bytes 15364
  41.8 12.3 %all-to-all-start = ((bf16[4,128,320]{1,2,0:T(8,128)(2,1)}), bf16[4,128,320]{1,2,0:T(8,128)(2,1)S(1)}, u32[]{:S(2)}, u32[]{:S(2)}) async-start(bf16[4,128,320]{1,2,0:T(8,128)(2,1)} %copy.51), calls=%async_computation | async-start | bytes 655360 | tf_op jit(solution)/shard_map/all_to_all | solution.py:120
  46.8 73.3 %all-gather.10.cloned.1.call-start = ((), (), s32[]{:S(2)}) async-start(), calls=%async_computation.7 | async-start | bytes 1638400 | tf_op jit(solution)/shard_map/all_gather | solution.py:130
  89.7 78.7 %reduce-scatter.3.cloned.1.call-start = ((), (), s32[]{:S(2)}) async-start(), calls=%async_computation.8 | async-start | bytes 2949120 | tf_op jit(solution)/shard_map/reduce_scatter | solution.py:134
  120.1 1.8 copy-start.14
  125.7 76.2 %all-gather.12.cloned.1.call-start = ((), (), s32[]{:S(2)}) async-start(), calls=%async_computation.9 | async-start | bytes 2949120 | tf_op jit(solution)/shard_map/all_gather | solution.py:138
  171.6 80.2 %reduce-scatter.5.cloned.1.call-start = ((), (), s32[]{:S(2)}) async-start(), calls=%async_computation.10 | async-start | bytes 2621440 | tf_op jit(solution)/shard_map/reduce_scatter | solution.py:140
  207.7 1.2 copy-start.11
  207.8 170.2 %all-gather.16.cloned.1.call-start = ((), (), s32[]{:S(2)}) async-start(), calls=%async_computation.12 | async-start | bytes 5242880 | tf_op jit(solution)/shard_map/all_gather | solution.py:93
  208.3 250.5 %all-gather.14.cloned.1.call-start = ((), (), s32[]{:S(2)}) async-start(), calls=%async_computation.11 | async-start | bytes 5242880 | tf_op jit(solution)/shard_map/all_gather | solution.py:163
  277.5 5.5 copy-start.13
  277.5 211.6 %all-to-all-start.3 = ((bf16[128,4,2048]{0,2,1:T(8,128)(2,1)}), bf16[128,4,2048]{0,2,1:T(8,128)(2,1)S(1)}, u32[]{:S(2)}, u32[]{:S(2)}) async-start(bf16[128,4,2048]{0,2,1:T(8,128)(2,1)} %bitcast.106), calls=%async_computation.5 | async-start | bytes 4194304 | tf_op jit(solution)/shard_map/all_to_all | solution.py:95
  281.2 252.2 %all-gather.18.cloned.1.call-start = ((), (), s32[]{:S(2)}) async-start(), calls=%async_computation.13 | async-start | bytes 2621440 | tf_op jit(solution)/shard_map/all_gather | solution.py:215
  283.1 180.9 %copy-start.9 = (f32[8192]{0:T(1024)S(1)}, f32[8192]{0:T(1024)}, u32[]{:S(2)}) copy-start(f32[8192]{0:T(1024)} %param.31) | copy-start | bytes 98308
  464.0 1.9 copy-start.4
  465.9 1.9 copy-start.2
  476.5 5.4 copy-start.3
  476.5 5.9 copy-start.5
  488.8 135.3 %all-gather.20.cloned.1.call-start = ((), (), s32[]{:S(2)}) async-start(), calls=%async_computation.14 | async-start | bytes 18874368 | tf_op jit(solution)/shard_map/all_gather | solution.py:102
  624.1 12.2 %copy-start.1 = (bf16[1280,1024]{1,0:T(8,128)(2,1)S(1)}, bf16[1280,1024]{1,0:T(8,128)(2,1)}, u32[]{:S(2)}) copy-start(bf16[1280,1024]{1,0:T(8,128)(2,1)} %param.27) | copy-start | bytes 7864324
Sparse Core Ops, SparseCore 0:
  10.2 63.4 all-gather.7
  89.8 30.1 all-gather.9
  125.8 42.6 reduce-scatter.2
  171.7 30.0 all-gather.11
  207.9 43.8 reduce-scatter.4
  253.3 124.6 all-gather.15
  379.7 79.1 all-gather.13
  489.0 44.4 all-gather.17
  535.5 88.5 all-gather.19
